TPU v7x, 32 devices: a whole 2x2x4 slice. The times are simulated.
32 devices in a mesh: groups: 2 (over y), wide: 4 (over z), narrow: 2 (over x), inner: 2 (over core).
Axes of the slice: x: 2, y: 2, z: 4, core: 2. Of those that a mesh axis runs over, the one named last changes fastest.
Arguments:
- centres: bfloat16 [12288, 768], P(('groups', 'wide', 'narrow')), parts along dimension 0, may hold values from -6 to 6
- weights: float32 [12288, 1000], P(('groups', 'wide', 'narrow'), 'inner'), parts along dimension 0, may hold values from -0.625 to 0.625
- pool_points: bfloat16 [1024, 768], P(('groups', 'wide', 'narrow')), parts along dimension 0, may hold values from -6 to 6
- pool_labels: bfloat16 [1024, 1000], P(('groups', 'wide', 'narrow'), 'inner'), parts along dimension 0, may hold values from -6 to 6
- batch_index: int32 [8, 8], P('groups', ('wide', 'narrow')), parts along dimension 0, may hold values from 0 to 63
- landmark_index: int32 [8192], P(('groups', 'wide', 'narrow')), parts along dimension 0, may hold values from 0 to 767
- eigvecs: float32 [8192, 160], P(('groups', 'wide', 'narrow')), parts along dimension 0, may hold values from -0.09375 to 0.09375
- eig_scale: float32 [320], P('groups'), parts along dimension 0, may hold values from 2 to 20
Outputs:
- descent: float32 [12288, 1000], P(('groups', 'wide', 'narrow'), 'inner'), parts along dimension 0
- residual: float32 [16, 1000], P('groups', 'inner'), parts along dimension 0
There are 2 independent parts, one for each index of `groups`. A program takes and returns all parts, laid end to end along the dimension named above; each array names one. Nothing has to cross between parts.
All inputs are finite; a program needn't handle non-finite values.
Results may differ from a plain program's by a relative error of at most 0.0003.
Values may be sent and summed in bfloat16 or wider, within the bound.
A program may use at most 64 MiB of HBM per device.

v0:
```python
import math

import jax
import jax.numpy as jnp
from jax import lax
from jax.sharding import PartitionSpec as P


def squared_norms(points):
    widened = points.astype(jnp.float32)
    return jnp.sum(widened * widened, axis=1)


def kernel_block(centre_rows, centre_norms, batch_points, batch_norms, spread):
    dot_terms = lax.dot_general(
        centre_rows, batch_points, (((1,), (1,)), ((), ())), preferred_element_type=jnp.float32
    )
    squared = centre_norms[:, None] + batch_norms[None, :] - 2.0 * dot_terms
    return jnp.exp(-jnp.sqrt(squared) / spread)


def body(
    centres, weights, pool_points, pool_labels, batch_index, landmark_index, eigvecs, eig_scale
):
    shards = lax.axis_size(("wide", "narrow"))
    width = centres.shape[1]
    spread = math.sqrt(0.5 * width)
    per_device = batch_index.shape[1]
    steps_total = batch_index.shape[0]
    step_size = 32.0 / (centres.shape[0] * shards * per_device * shards)
    centre_norms = squared_norms(centres)
    descent = jnp.zeros(weights.shape, jnp.float32)
    residual = jnp.zeros((per_device * shards, weights.shape[1]), jnp.float32)
    for step_index in range(steps_total):
        own_points = jnp.take(pool_points, batch_index[step_index], axis=0)
        own_labels = jnp.take(pool_labels, batch_index[step_index], axis=0)
        batch_points, batch_labels = (
            lax.all_gather(own_points, ("wide", "narrow"), axis=0, tiled=True),
            lax.all_gather(own_labels, ("wide", "narrow"), axis=0, tiled=True),
        )
        batch_norms = squared_norms(batch_points)
        kernel = kernel_block(centres, centre_norms, batch_points, batch_norms, spread)
        partial_pred = lax.dot_general(
            kernel,
            weights,
            (((0,), (0,)), ((), ())),
            precision=lax.Precision.HIGHEST,
            preferred_element_type=jnp.float32,
        )
        predicted = lax.psum(partial_pred, ("wide", "narrow"))
        residual = predicted - batch_labels.astype(jnp.float32)
        gradient = jnp.dot(
            kernel, residual, precision=lax.Precision.HIGHEST, preferred_element_type=jnp.float32
        )
        local_terms = lax.dot_general(
            eigvecs,
            jnp.take(gradient, landmark_index, axis=0),
            (((0,), (0,)), ((), ())),
            precision=lax.Precision.HIGHEST,
            preferred_element_type=jnp.float32,
        )
        coefficients = lax.psum(local_terms, ("wide", "narrow"))
        correction_rows = jnp.dot(
            eigvecs,
            eig_scale[:, None] * coefficients,
            precision=lax.Precision.HIGHEST,
            preferred_element_type=jnp.float32,
        )
        correction = gradient.at[landmark_index].add(-correction_rows)
        weights = weights - step_size * correction
        descent = descent + correction
    return (descent, residual)


def solution(mesh):
    return jax.shard_map(
        body,
        mesh=mesh,
        in_specs=(
            P(("groups", "wide", "narrow"), None),
            P(("groups", "wide", "narrow"), "inner"),
            P(("groups", "wide", "narrow"), None),
            P(("groups", "wide", "narrow"), "inner"),
            P("groups", ("wide", "narrow")),
            P(("groups", "wide", "narrow")),
            P(("groups", "wide", "narrow"), None),
            P("groups"),
        ),
        out_specs=(P(("groups", "wide", "narrow"), "inner"), P("groups", "inner")),
        check_vma=False,
    )
```

profile of v0, /device:TPU:0, one launch (start us, length us, event | category | flops | bytes accessed | tf_op | source)
XLA Modules:
  0.0 698.4 jit_solution(2187172956093595467)
XLA Ops:
  18.4 32.1 %all-gather = bf16[8,1,768]{2,1,0:T(2,128)(2,1)S(1)} all-gather(bf16[1,1,768]{2,1,0:T(2,128)(2,1)S(1)} %get-tuple-element.33), channel_id=1, replica_groups=mesh['groups'=2,'wide'=4,'narrow'=2,'inner'=2] {'wide','narrow'}, dimensions={0}, use_global_device_ids=true | all-gather | bytes 13824 | tf_op jit(solution)/shard_map/all_gather | solution.py:38
  50.6 1.6 multiply_reduce_fusion
  52.2 1.7 fusion.30
  55.3 36.9 %psum.56 = f32[8,500]{1,0:T(8,128)S(1)} all-reduce(f32[8,500]{1,0:T(8,128)S(1)} %fusion.86), channel_id=1, replica_groups=mesh['groups'=2,'wide'=4,'narrow'=2,'inner'=2] {'wide','narrow'}, use_global_device_ids=true, to_apply=%region_2.4 | all-reduce | flops 4000 | bytes 32000 | tf_op jit(solution)/shard_map/psum | solution.py:50
  93.0 26.0 %all-gather.1 = bf16[8,1,500]{2,1,0:T(2,128)(2,1)S(1)} all-gather(bf16[1,1,500]{2,1,0:T(2,128)(2,1)S(1)} %get-tuple-element.39), channel_id=1, replica_groups=mesh['groups'=2,'wide'=4,'narrow'=2,'inner'=2] {'wide','narrow'}, dimensions={0}, use_global_device_ids=true | all-gather | bytes 9000 | tf_op jit(solution)/shard_map/all_gather | solution.py:39
  120.5 1.6 gather_fusion
  122.1 1.6 convolution_bitcast_fusion.3
  123.9 3.1 copy.48
  127.0 30.3 %all-gather.2 = bf16[8,1,768]{2,1,0:T(2,128)(2,1)S(1)} all-gather(bf16[1,1,768]{2,1,0:T(2,128)(2,1)S(1)} %get-tuple-element.34), channel_id=1, replica_groups=mesh['groups'=2,'wide'=4,'narrow'=2,'inner'=2] {'wide','narrow'}, dimensions={0}, use_global_device_ids=true | all-gather | bytes 13824 | tf_op jit(solution)/shard_map/all_gather | solution.py:38
  157.3 26.9 %all-gather.3 = bf16[8,1,500]{2,1,0:T(2,128)(2,1)} all-gather(bf16[1,1,500]{2,1,0:T(2,128)(2,1)S(1)} %get-tuple-element.38), channel_id=1, replica_groups=mesh['groups'=2,'wide'=4,'narrow'=2,'inner'=2] {'wide','narrow'}, dimensions={0}, use_global_device_ids=true | all-gather | bytes 9000 | tf_op jit(solution)/shard_map/all_gather | solution.py:39
  184.2 30.3 %all-gather.4 = bf16[8,1,768]{2,1,0:T(2,128)(2,1)S(1)} all-gather(bf16[1,1,768]{2,1,0:T(2,128)(2,1)S(1)} %get-tuple-element.36), channel_id=1, replica_groups=mesh['groups'=2,'wide'=4,'narrow'=2,'inner'=2] {'wide','narrow'}, dimensions={0}, use_global_device_ids=true | all-gather | bytes 13824 | tf_op jit(solution)/shard_map/all_gather | solution.py:38
  214.5 26.6 %all-gather.5 = bf16[8,1,500]{2,1,0:T(2,128)(2,1)} all-gather(bf16[1,1,500]{2,1,0:T(2,128)(2,1)S(1)} %get-tuple-element.40), channel_id=1, replica_groups=mesh['groups'=2,'wide'=4,'narrow'=2,'inner'=2] {'wide','narrow'}, dimensions={0}, use_global_device_ids=true | all-gather | bytes 9000 | tf_op jit(solution)/shard_map/all_gather | solution.py:39
  241.0 30.3 %all-gather.6 = bf16[8,1,768]{2,1,0:T(2,128)(2,1)S(1)} all-gather(bf16[1,1,768]{2,1,0:T(2,128)(2,1)S(1)} %get-tuple-element.35), channel_id=1, replica_groups=mesh['groups'=2,'wide'=4,'narrow'=2,'inner'=2] {'wide','narrow'}, dimensions={0}, use_global_device_ids=true | all-gather | bytes 13824 | tf_op jit(solution)/shard_map/all_gather | solution.py:38
  271.4 26.7 %all-gather.7 = bf16[8,1,500]{2,1,0:T(2,128)(2,1)} all-gather(bf16[1,1,500]{2,1,0:T(2,128)(2,1)S(1)} %get-tuple-element.37), channel_id=1, replica_groups=mesh['groups'=2,'wide'=4,'narrow'=2,'inner'=2] {'wide','narrow'}, dimensions={0}, use_global_device_ids=true | all-gather | bytes 9000 | tf_op jit(solution)/shard_map/all_gather | solution.py:39
  298.7 2.1 fusion.6
  302.2 5.0 scatter_fusion
  308.7 34.0 %psum.58 = f32[8,500]{1,0:T(8,128)} all-reduce(f32[8,500]{1,0:T(8,128)} %fusion.36), channel_id=1, replica_groups=mesh['groups'=2,'wide'=4,'narrow'=2,'inner'=2] {'wide','narrow'}, use_global_device_ids=true, to_apply=%region_6.10 | all-reduce | flops 4000 | bytes 32000 | tf_op jit(solution)/shard_map/psum | solution.py:50
  342.8 2.2 fusion.54
  344.9 2.5 gather_fusion.1
  347.4 2.9 convolution_bitcast_fusion.2
  350.5 1.7 fusion.18
  352.2 66.5 %all-reduce.7.cloned.1.call-done = f32[160,500]{1,0:T(8,128)} async-done(((f32[160,500]{1,0:T(8,128)}), f32[160,500]{1,0:T(8,128)}) %all-reduce.7.cloned.1.call-update) | async-done | bytes 320016 | tf_op jit(solution)/shard_map/psum | solution.py:62
  418.7 3.1 fusion.5
  421.8 2.5 copy.52
  424.3 4.8 scatter_fusion.1
  429.2 3.1 fusion.84
  432.3 35.4 %psum.60 = f32[8,500]{1,0:T(8,128)S(1)} all-reduce(f32[8,500]{1,0:T(8,128)} %fusion.84), channel_id=1, replica_groups=mesh['groups'=2,'wide'=4,'narrow'=2,'inner'=2] {'wide','narrow'}, use_global_device_ids=true, to_apply=%region_10.14 | all-reduce | flops 4000 | bytes 32000 | tf_op jit(solution)/shard_map/psum | solution.py:50
  467.7 3.3 fusion.53
  471.0 4.1 gather_fusion.2
  475.1 2.9 convolution_bitcast_fusion.1
  478.4 1.7 fusion.12
  480.2 1.6 copy.53
  481.8 1.6 copy.54
  483.4 63.1 %all-reduce.9.cloned.1.call-done = f32[160,500]{1,0:T(8,128)} async-done(((f32[160,500]{1,0:T(8,128)}), f32[160,500]{1,0:T(8,128)}) %all-reduce.9.cloned.1.call-update) | async-done | bytes 320016 | tf_op jit(solution)/shard_map/psum | solution.py:62
  546.5 3.1 fusion.4
  549.6 2.5 copy.58
  552.1 6.7 scatter_fusion.2
  558.9 3.0 copy.59
  561.9 3.1 fusion
  565.0 35.3 %psum.62 = f32[8,500]{1,0:T(8,128)S(1)} all-reduce(f32[8,500]{1,0:T(8,128)S(1)} %fusion), channel_id=1, replica_groups=mesh['groups'=2,'wide'=4,'narrow'=2,'inner'=2] {'wide','narrow'}, use_global_device_ids=true, to_apply=%region_14.18 | all-reduce | flops 4000 | bytes 32000 | tf_op jit(solution)/shard_map/psum | solution.py:50
  600.3 5.0 add_add_fusion
  605.3 1.9 copy.61
  607.2 2.3 gather_fusion.3
  609.5 2.9 convolution_bitcast_fusion
  612.8 67.9 %all-reduce.11.cloned.1.call-done = f32[160,500]{1,0:T(8,128)} async-done(((f32[160,500]{1,0:T(8,128)}), f32[160,500]{1,0:T(8,128)}) %all-reduce.11.cloned.1.call-update) | async-done | bytes 320016 | tf_op jit(solution)/shard_map/psum | solution.py:62
  680.7 3.1 fusion.3
  685.4 4.4 scatter_fusion.3
  689.8 1.6 copy.64
  (57 shorter events, 13.6 us)
Async XLA Ops:
  7.2 114.9 %copy-start = (f32[512,160]{0,1:T(8,128)S(1)}, f32[512,160]{0,1:T(8,128)}, u32[]{:S(2)}) copy-start(f32[512,160]{0,1:T(8,128)} %param.20) | copy-start | bytes 983044
  7.2 46.7 %copy-start.3 = (f32[768,500]{0,1:T(8,128)S(1)}, f32[768,500]{0,1:T(8,128)}, u32[]{:S(2)}) copy-start(f32[768,500]{0,1:T(8,128)} %param.15) | copy-start | bytes 4608004
  7.2 291.5 %all-reduce.5.cloned.1.call-start = ((), (), s32[]{:S(2)}) async-start(), calls=%async_computation | async-start | bytes 655360 | tf_op jit(solution)/shard_map/psum | solution.py:62
  17.5 104.5 %copy-start.11 = (pred[512]{0:T(512)(128)(4,1)}, pred[512]{0:T(512)(128)(4,1)S(1)}, u32[]{:S(2)}) copy-start(pred[512]{0:T(512)(128)(4,1)S(1)} %compare_and_fusion) | copy-start | bytes 1540
  119.0 3.1 copy-start.6
  123.8 174.4 %copy-start.1 = (bf16[768,768]{1,0:T(8,128)(2,1)S(1)}, bf16[768,768]{1,0:T(8,128)(2,1)}, u32[]{:S(2)}) copy-start(bf16[768,768]{1,0:T(8,128)(2,1)} %param.14) | copy-start | bytes 3538948
  123.8 174.9 %copy-start.9 = (f32[160]{0:T(256)S(1)}, f32[160]{0:T(256)}, u32[]{:S(2)}) copy-start(f32[160]{0:T(256)} %param.21) | copy-start | bytes 1924
  123.8 294.9 %all-reduce.7.cloned.1.call-start = ((), (), s32[]{:S(2)}) async-start(), calls=%async_computation.1 | async-start | bytes 655360 | tf_op jit(solution)/shard_map/psum | solution.py:62
  302.2 5.0 copy-start.2
  344.9 2.5 copy-start.12
  350.3 196.2 %all-reduce.9.cloned.1.call-start = ((), (), s32[]{:S(2)}) async-start(), calls=%async_computation.2 | async-start | bytes 655360 | tf_op jit(solution)/shard_map/psum | solution.py:62
  432.3 38.7 %copy-start.7 = (s32[1024]{0:T(1024)S(1)}, s32[1024]{0:T(1024)}, u32[]{:S(2)}) copy-start(s32[1024]{0:T(1024)} %copy-done.6) | copy-start | bytes 12292
  471.0 4.1 copy-start.13
  478.0 202.7 %all-reduce.11.cloned.1.call-start = ((), (), s32[]{:S(2)}) async-start(), calls=%async_computation.3 | async-start | bytes 655360 | tf_op jit(solution)/shard_map/psum | solution.py:62
  481.8 64.7 %copy-start.10 = (f32[160]{0:T(256)S(1)}, f32[160]{0:T(256)}, u32[]{:S(2)}) copy-start(f32[160]{0:T(256)} %param.21) | copy-start | bytes 1924
  561.9 38.4 %copy-start.5 = (bf16[8,1,500]{2,1,0:T(2,128)(2,1)S(1)}, bf16[8,1,500]{2,1,0:T(2,128)(2,1)}, u32[]{:S(2)}) copy-start(bf16[8,1,500]{2,1,0:T(2,128)(2,1)} %all-gather.7) | copy-start | bytes 24004
  600.3 5.0 copy-start.4
  605.3 1.9 copy-start.8
  607.1 2.3 copy-start.14
Sparse Core Ops, SparseCore 0:
  123.9 68.4 all-reduce.4
  350.4 68.2 all-reduce.6
  478.2 68.2 all-reduce.8
  612.5 68.2 all-reduce.10
where the time goes:
time: 708 us; the launch traced here: 698 us
  blocking collectives  371 us (52%)
  waiting for transfers between devices  198 us (28%)
  matrix products  48.3 us (7%)
  local copies, waits for them, and re-layouts  33.3 us (5%)
  other arithmetic  26 us (4%)
  between operations  22 us (3%)
    psum x4, waiting for transfers between devices, body(): coefficients = lax.psum(local_terms, ('wide', 'narrow'))  198 us
    psum x4, blocking collectives, body(): predicted = lax.psum(partial_pred, ('wide', 'narrow'))  142 us
    all_gather x4, blocking collectives, body(): lax.all_gather(own_points, ('wide', 'narrow'), axis=0, tiled=True)  123 us
    all_gather x4, blocking collectives, body(): lax.all_gather(own_labels, ('wide', 'narrow'), axis=0, tiled=True)  106 us
    scatter-add x4, other arithmetic, body(): correction = gradient.at[landmark_index].add(-correction_rows)  21 us
  transfers between devices with their start and end apart: 4, of which 3 were waited for; matrix products, arithmetic and copies ran while one was open for 2% of the time, Pallas kernels for 0%

commit v1 on v0

v1 whole, which is shorter than its diff:
```python
import functools
import math

import jax
import jax.numpy as jnp
from jax import lax
from jax.experimental import pallas as pl
from jax.experimental.pallas import tpu as pltpu
from jax.sharding import PartitionSpec as P

MESH = pl.DeviceIdType.MESH
F32, BF16, I32 = jnp.float32, jnp.bfloat16, jnp.int32
LANES = 128
ROWS_PER_STEP = 8
VMEM_BYTES = 40 * 1024 * 1024

NN = (((1,), (0,)), ((), ()))
NT = (((1,), (1,)), ((), ()))
TN = (((0,), (0,)), ((), ()))


def dot(a, b, dims):
    return lax.dot_general(a, b, dims, preferred_element_type=F32)


def split(x):
    head = x.astype(BF16)
    return head, (x - head.astype(F32)).astype(BF16)


def dot_split(a_parts, b_parts, dims):
    a_head, a_rest = a_parts
    b_head, b_rest = b_parts
    rows = a_head.shape[0]
    both = dot(jnp.concatenate([a_head, a_rest], axis=0), b_head, dims)
    return both[:rows] + (both[rows:] + dot(a_head, b_rest, dims))


def iota(shape, dim):
    return lax.broadcasted_iota(I32, shape, dim)


def steps_kernel(
    narrow, shards, steps, spread, step_size,
    bidx_ref, lidx_hbm, scale_hbm, centres_hbm, weights_hbm, pool_hbm, labels_hbm, eig_hbm,
    mt_ref, r_ref,
    lidx, scale, centres, weights, pool, labels, eig,
    w_head, w_rest, e_head, e_rest,
    own_pts, all_pts, x, x_in, ag,
    load_sem, pts_send, pts_recv, x_send, x_recv, ag_send, ag_recv,
):
    me = lax.axis_index("wide") * narrow + lax.axis_index("narrow")
    peers = [lax.rem(me + k, shards) for k in range(1, shards)]

    def at(peer):
        return {"wide": peer // narrow, "narrow": lax.rem(peer, narrow)}

    barrier = pltpu.get_barrier_semaphore()
    for peer in peers:
        pl.semaphore_signal(barrier, inc=1, device_id=at(peer), device_id_type=MESH)

    loads = {}
    for place, (name, src, dst) in enumerate((
        ("pool", pool_hbm, pool),
        ("lidx", lidx_hbm, lidx),
        ("eig", eig_hbm, eig),
        ("centres", centres_hbm, centres),
        ("labels", labels_hbm, labels),
        ("scale", scale_hbm, scale),
        ("weights", weights_hbm, weights),
    )):
        loads[name] = pltpu.make_async_copy(src, dst, load_sem.at[place])
        loads[name].start()

    total = steps * shards
    count, width = centres.shape
    outs = weights.shape[1]
    eigs = eig.shape[1]
    pool_rows = pool.shape[0]
    pieces = width // LANES
    half = x.shape[2]
    w_cols = 2 * half - 256
    b_col = w_cols + eigs - half

    loads["pool"].wait()
    stacked = jnp.concatenate(
        [pool[:, LANES * q:LANES * (q + 1)] for q in range(pieces)], axis=0
    )
    pack_rows = own_pts.shape[0]
    shape = (pack_rows, pieces * pool_rows)
    row, col = iota(shape, 0), iota(shape, 1)
    wanted = row // steps * pool_rows
    step_of = row % steps
    for s in range(steps):
        wanted = wanted + jnp.where(step_of == s, bidx_ref[0, s], 0)
    own = dot(jnp.where(row // steps < pieces, jnp.where(col == wanted, 1.0, 0.0), 0.0).astype(BF16), stacked, NN)
    own_pts[...] = own.astype(BF16)

    pl.semaphore_wait(barrier, shards - 1)
    pts_copies = []
    for peer in peers:
        copy = pltpu.make_async_remote_copy(
            src_ref=own_pts, dst_ref=all_pts.at[me],
            send_sem=pts_send.at[peer], recv_sem=pts_recv.at[me],
            device_id=at(peer), device_id_type=MESH,
        )
        copy.start()
        pts_copies.append(copy)
    all_pts[pl.ds(me, 1)] = own_pts[...][None]
    x[...] = jnp.zeros_like(x)

    loads["lidx"].wait()
    loads["eig"].wait()
    marks = lidx.shape[1]
    chosen = jnp.where(iota((count, marks), 0) == lidx[...], 1.0, 0.0).astype(BF16)
    eig_head, eig_rest = split(eig[...])
    placed = dot(chosen, eig_head, NN) + dot(chosen, eig_rest, NN)
    e_parts = split(placed)
    e_head[...], e_rest[...] = e_parts

    loads["centres"].wait()
    sums = jnp.zeros((count, LANES), F32)
    for q in range(pieces):
        piece = centres[:, LANES * q:LANES * (q + 1)].astype(F32)
        sums = sums + piece * piece
    s_head, s_rest = split(sums)
    s_tail = (sums - s_head.astype(F32) - s_rest.astype(F32)).astype(BF16)
    ones = jnp.ones((16, LANES), BF16)
    centre_norms = (dot(ones, s_head, NT) + (dot(ones, s_rest, NT) + dot(ones, s_tail, NT)))[0:1]

    loads["labels"].wait()
    shape = (total, pool_rows)
    row, col = iota(shape, 0), iota(shape, 1)
    wanted = jnp.zeros(shape, I32)
    for s in range(steps):
        wanted = wanted + jnp.where(row // shards == s, bidx_ref[0, s], 0)
    pick = jnp.where(row % shards == me, jnp.where(col == wanted, 1.0, 0.0), 0.0).astype(BF16)
    label_rows = dot(pick, labels[...], NN)

    loads["scale"].wait()
    loads["weights"].wait()
    w_parts = split(weights[...])
    w_head[...], w_rest[...] = w_parts

    shape = (pieces * total, shards * pack_rows)
    row, col = iota(shape, 0), iota(shape, 1)
    source = row % shards * pack_rows + row // total * steps + row % total // shards
    order = jnp.where(col == source, 1.0, 0.0).astype(BF16)

    for copy in pts_copies:
        copy.wait_send()
    for peer in peers:
        pltpu.make_async_remote_copy(
            src_ref=own_pts, dst_ref=all_pts.at[peer],
            send_sem=pts_send.at[peer], recv_sem=pts_recv.at[peer],
            device_id=at(peer), device_id_type=MESH,
        ).wait_recv()
    ordered = dot(order, all_pts[...].reshape(shards * pack_rows, LANES), NN)
    points = jnp.concatenate([ordered[total * q:total * (q + 1)] for q in range(pieces)], axis=1)
    point_norms = jnp.sum(points * points, axis=1, keepdims=True)
    dots = dot(points.astype(BF16), centres[...], NT)
    squared = jnp.maximum(centre_norms + point_norms - 2.0 * dots, 0.0)
    kernel = jnp.exp(jnp.sqrt(squared) * (-1.0 / spread))

    k_parts = split(kernel)
    x_w = dot_split(k_parts, (w_head[...], w_rest[...]), NN) - label_rows
    x_e = dot_split(k_parts, (e_head[...], e_rest[...]), NN)
    x_k = dot_split(k_parts, k_parts, NT)
    for s in range(steps):
        rows = slice(shards * s, shards * (s + 1))
        x[2 * s] = x_w[rows, :half]
        x[2 * s + 1, :, :outs - half] = x_w[rows, half:]
        x[2 * s + 1, :, w_cols - half:b_col] = x_e[rows]
        x[2 * s + 1, :, b_col:b_col + total] = x_k[rows]

    x_copies = []
    for peer in peers:
        copy = pltpu.make_async_remote_copy(
            src_ref=x.at[peer], dst_ref=x_in.at[me],
            send_sem=x_send.at[peer], recv_sem=x_recv.at[me],
            device_id=at(peer), device_id_type=MESH,
        )
        copy.start()
        x_copies.append(copy)
    summed = x[pl.ds(me, 1)][0]
    for peer in peers:
        pltpu.make_async_remote_copy(
            src_ref=x.at[peer], dst_ref=x_in.at[peer],
            send_sem=x_send.at[peer], recv_sem=x_recv.at[peer],
            device_id=at(peer), device_id_type=MESH,
        ).wait_recv()
        summed = summed + x_in[pl.ds(peer, 1)][0]
    ag[pl.ds(me, 1)] = summed[None]
    ag_copies = []
    for peer in peers:
        copy = pltpu.make_async_remote_copy(
            src_ref=ag.at[me], dst_ref=ag.at[me],
            send_sem=ag_send.at[peer], recv_sem=ag_recv.at[me],
            device_id=at(peer), device_id_type=MESH,
        )
        copy.start()
        ag_copies.append(copy)
    for copy in x_copies:
        copy.wait_send()
    for peer in peers:
        pltpu.make_async_remote_copy(
            src_ref=ag.at[peer], dst_ref=ag.at[peer],
            send_sem=ag_send.at[peer], recv_sem=ag_recv.at[peer],
            device_id=at(peer), device_id_type=MESH,
        ).wait_recv()
    for copy in ag_copies:
        copy.wait_send()

    left = [ag[2 * s] for s in range(steps)]
    right = [ag[2 * s + 1] for s in range(steps)]
    rights = jnp.concatenate(right, axis=0)
    coeffs = rights[:, w_cols - half:b_col]
    gram = rights[:, b_col:b_col + total]
    scaled = split(coeffs * scale[...])
    coupling = (gram - dot_split(scaled, split(coeffs), NT)) * step_size
    mt_ref[...] = kernel - dot_split(scaled, (e_head[...], e_rest[...]), NT)

    rests = [
        jnp.concatenate([left[s], right[s][:, :w_cols - half]], axis=1) for s in range(steps)
    ]
    for s in range(steps):
        known = rests[s]
        for later in range(s + 1, steps):
            factors = coupling[shards * later:shards * (later + 1), shards * s:shards * (s + 1)]
            moved = rests[later]
            for j in range(shards):
                moved = moved - factors[:, j:j + 1] * known[j:j + 1, :]
            rests[later] = moved
        r_ref[shards * s:shards * (s + 1), :] = known


def apply_kernel(outs, last, mt_ref, r_ref, descent_ref, residual_ref):
    m_head, m_rest = split(mt_ref[...])
    r_all = r_ref[...][:, :outs]
    r_head, r_rest = split(r_all)
    lhs = jnp.concatenate([m_head, m_rest, m_head], axis=0)
    rhs = jnp.concatenate([r_head, r_head, r_rest], axis=0)
    descent_ref[...] = dot(lhs, rhs, TN)
    residual_ref[...] = r_all[last:]


def fused_body(
    narrow, shards,
    centres, weights, pool_points, pool_labels, batch_index, landmark_index, eigvecs, eig_scale
):
    steps = batch_index.shape[0]
    count, width = centres.shape
    outs = weights.shape[1]
    marks, eigs = eigvecs.shape
    pool_rows = pool_points.shape[0]
    spread = math.sqrt(0.5 * width)
    step_size = 32.0 / (count * shards * shards)
    total = steps * shards
    padded = -(-outs // LANES) * LANES
    half = (padded + 256) // 2
    pack_rows = -(-(steps * width // LANES) // 16) * 16
    any_spec = pl.BlockSpec(memory_space=pl.ANY)
    vmem_spec = pl.BlockSpec(memory_space=pltpu.VMEM)
    mt, r = pl.pallas_call(
        functools.partial(steps_kernel, narrow, shards, steps, spread, step_size),
        out_shape=(
            jax.ShapeDtypeStruct((total, count), F32),
            jax.ShapeDtypeStruct((total, padded), F32),
        ),
        in_specs=[pl.BlockSpec(memory_space=pltpu.SMEM)] + [any_spec] * 7,
        out_specs=(vmem_spec, vmem_spec),
        scratch_shapes=[
            pltpu.VMEM((1, marks), I32),
            pltpu.VMEM((1, eigs), F32),
            pltpu.VMEM((count, width), BF16),
            pltpu.VMEM((count, outs), F32),
            pltpu.VMEM((pool_rows, width), BF16),
            pltpu.VMEM((pool_rows, outs), BF16),
            pltpu.VMEM((marks, eigs), F32),
            pltpu.VMEM((count, outs), BF16),
            pltpu.VMEM((count, outs), BF16),
            pltpu.VMEM((count, eigs), BF16),
            pltpu.VMEM((count, eigs), BF16),
            pltpu.VMEM((pack_rows, LANES), BF16),
            pltpu.VMEM((shards, pack_rows, LANES), BF16),
            pltpu.VMEM((shards, ROWS_PER_STEP, half), F32),
            pltpu.VMEM((shards, ROWS_PER_STEP, half), F32),
            pltpu.VMEM((shards, ROWS_PER_STEP, half), F32),
            pltpu.SemaphoreType.DMA((7,)),
        ] + [pltpu.SemaphoreType.DMA((shards,))] * 6,
        compiler_params=pltpu.CompilerParams(
            collective_id=0, has_side_effects=True, vmem_limit_bytes=VMEM_BYTES
        ),
    )(
        batch_index.reshape(1, steps), landmark_index.reshape(1, marks),
        eig_scale.reshape(1, eigs), centres, weights, pool_points, pool_labels, eigvecs,
    )
    block = count // 3 if count % 384 == 0 else count
    return pl.pallas_call(
        functools.partial(apply_kernel, outs, total - shards),
        grid=(count // block,),
        out_shape=(
            jax.ShapeDtypeStruct((count, outs), F32),
            jax.ShapeDtypeStruct((shards, outs), F32),
        ),
        in_specs=[
            pl.BlockSpec((total, block), lambda i: (0, i)),
            pl.BlockSpec((total, padded), lambda i: (0, 0)),
        ],
        out_specs=(
            pl.BlockSpec((block, outs), lambda i: (i, 0)),
            pl.BlockSpec((shards, outs), lambda i: (0, 0)),
        ),
        compiler_params=pltpu.CompilerParams(vmem_limit_bytes=VMEM_BYTES),
    )(mt, r)


def plain_body(
    centres, weights, pool_points, pool_labels, batch_index, landmark_index, eigvecs, eig_scale
):
    axes = ("wide", "narrow")
    shards = lax.axis_size(axes)
    me = lax.axis_index(axes)
    steps, per_device = batch_index.shape
    batch = shards * per_device
    count, width = centres.shape
    outs = weights.shape[1]
    spread = math.sqrt(0.5 * width)
    step_size = 32.0 / (count * shards * batch)
    exact = functools.partial(
        lax.dot_general, precision=lax.Precision.HIGHEST, preferred_element_type=F32
    )
    own_points = jnp.take(pool_points, batch_index, axis=0)
    own_labels = jnp.take(pool_labels, batch_index, axis=0)
    points = lax.all_gather(own_points, axes, axis=1, tiled=True).reshape(steps * batch, width)
    wide_points = points.astype(F32)
    wide_centres = centres.astype(F32)
    point_norms = jnp.sum(wide_points * wide_points, axis=1, keepdims=True)
    centre_norms = jnp.sum(wide_centres * wide_centres, axis=1)[None]
    squared = centre_norms + point_norms - 2.0 * dot(points, centres, NT)
    kernel = jnp.exp(-jnp.sqrt(jnp.maximum(squared, 0.0)) / spread)
    placed = jnp.zeros((count, eigvecs.shape[1]), F32).at[landmark_index].add(eigvecs)
    labels = lax.dynamic_update_slice(
        jnp.zeros((steps, batch, outs), F32), own_labels.astype(F32), (0, me * per_device, 0)
    )
    predicted = exact(kernel, weights, NN) - labels.reshape(steps * batch, outs)
    predicted, coeffs, gram = lax.psum(
        (predicted, exact(kernel, placed, NN), exact(kernel, kernel, NT)), axes
    )
    scaled = coeffs * eig_scale[None]
    coupling = (gram - exact(scaled, coeffs, NT)) * step_size
    mixed = kernel - exact(scaled, placed, NT)
    known = predicted[:batch]
    for s in range(1, steps):
        rows = slice(batch * s, batch * (s + 1))
        fresh = predicted[rows] - exact(coupling[rows, :batch * s], known, NN)
        known = jnp.concatenate([known, fresh], axis=0)
    return exact(mixed, known, TN), known[-batch:]


def solution(mesh):
    narrow = mesh.shape["narrow"]
    shards = mesh.shape["wide"] * narrow

    def body(*args):
        centres, weights = args[0], args[1]
        steps, per_device = args[4].shape
        fits = (
            shards == ROWS_PER_STEP and 2 * steps == shards and per_device == 1
            and centres.shape[1] % LANES == 0 and args[6].shape[1] + steps * shards <= 256
        )
        if fits:
            return fused_body(narrow, shards, *args)
        return plain_body(*args)

    return jax.shard_map(
        body,
        mesh=mesh,
        in_specs=(
            P(("groups", "wide", "narrow"), None),
            P(("groups", "wide", "narrow"), "inner"),
            P(("groups", "wide", "narrow"), None),
            P(("groups", "wide", "narrow"), "inner"),
            P("groups", ("wide", "narrow")),
            P(("groups", "wide", "narrow")),
            P(("groups", "wide", "narrow"), None),
            P("groups"),
        ),
        out_specs=(P(("groups", "wide", "narrow"), "inner"), P("groups", "inner")),
        check_vma=False,
    )
```

time: 708 us -> 27.6 us (0.04); the launches traced: 698 us -> 27.4 us
  blocking collectives: 371 us -> 0 us
  waiting for transfers between devices: 198 us -> 0 us
  matrix products: 48.3 us -> 0 us
  local copies, waits for them, and re-layouts: 33.3 us -> 4.77 us
  other arithmetic: 26 us -> 0 us
  Pallas kernels: 0 us -> 21.9 us
  between operations: 22 us -> 0.75 us
    all_gather x8 -> x0, blocking collectives: 229 us -> none  [the longest x4 123 us: body(): lax.all_gather(own_points, ('wide', 'narrow'), axis=0, tiled=True)]
    psum x4 -> x0, waiting for transfers between devices: 198 us -> none  [body(): coefficients = lax.psum(local_terms, ('wide', 'narrow'))]
    psum x4 -> x0, blocking collectives: 142 us -> none  [body(): predicted = lax.psum(partial_pred, ('wide', 'narrow'))]
    dot_general x20 -> x0, matrix products: 48.3 us -> none  [the longest x4 11.9 us: body(): jnp.dot(kernel, residual, precision=lax.Precision.HIGHEST, preferred_elem...]
    pallas_call x0 -> x2, Pallas kernels: none -> 21.9 us  [the longest x1 20.8 us: fused_body(): pl.pallas_call(functools.partial(steps_kernel, narrow, shards, steps, spr...]
    scatter-add x4 -> x0, other arithmetic: 21 us -> none  [body(): correction = gradient.at[landmark_index].add(-correction_rows)]
    gather x4 -> x0, local copies, waits for them, and re-layouts: 10.5 us -> none  [body(): jnp.take(gradient, landmark_index, axis=0)]
    neg x4 -> x0, local copies, waits for them, and re-layouts: 7.9 us -> none  [body(): correction = gradient.at[landmark_index].add(-correction_rows)]
  transfers between devices with their start and end apart: 4 -> 0, of which waited for: 3 -> 0; matrix products, arithmetic and copies ran while one was open for 2% -> 0% of each run, Pallas kernels for 0% -> 0%
where the time goes in v1:
time: 27.6 us; the launch traced here: 27.4 us
  Pallas kernels  21.9 us (79%)
  local copies, waits for them, and re-layouts  4.77 us (17%)
  between operations  0.75 us (3%)
    pallas_call x1, Pallas kernels, fused_body(): pl.pallas_call(functools.partial(steps_kernel, narrow, shards, steps, spr...  20.8 us
    unnamed x14, local copies, waits for them, and re-layouts  3.16 us
    pallas_call x1, local copies, waits for them, and re-layouts, fused_body(): pl.pallas_call(functools.partial(apply_kernel, outs, total - shards), gri...  1.6 us
    pallas_call x1, Pallas kernels, fused_body(): pl.pallas_call(functools.partial(apply_kernel, outs, total - shards), gri...  1.15 us

profile of v1, /device:TPU:0, one launch (start us, length us, event | category | flops | bytes accessed | tf_op | source)
XLA Modules:
  0.0 27.4 jit_solution(16496675767425918494)
XLA Ops:
  0.6 1.2 %copy.11.eig_hbm = f32[512,160]{1,0:T(8,128)S(1)} copy(f32[512,160]{0,1:T(8,128)} %param.14) | data formatting | bytes 655360 | tf_op args[6]
  1.8 0.0 copy-start
  1.8 0.0 copy-start.1
  1.8 0.0 copy-start.2
  1.8 0.0 copy-start.3
  1.9 0.0 copy-start.4
  1.9 0.0 copy-start.5
  1.9 2.0 %copy.10.weights_hbm = f32[768,500]{1,0:T(8,128)S(1)} copy(f32[768,500]{0,1:T(8,128)} %param.9) | data formatting | bytes 3072000 | tf_op args[1]
  3.8 0.0 copy-done
  3.9 0.0 copy-done.1
  3.9 0.0 copy-done.2
  3.9 0.0 copy-done.3
  3.9 0.0 copy-done.4
  3.9 0.0 copy-done.5
  3.9 20.8 %shard_map.95 = (f32[32,768]{1,0:T(8,128)S(1)}, f32[32,512]{1,0:T(8,128)S(1)}) custom-call(s32[1,4]{1,0:T(1,128)S(1)} %bitcast.5, s32[1,512]{1,0:T(1,128)S(1)} %bitcast.3, f32[1,160]{1,0:T(1,128)S(1)} %bitcast.4, bf16[768,768]{1,0:T(8,128)(2,1)S(1)} %copy-done, f32[768,500]{1,0:T(8,128)S(1)} %copy.10.weights_hbm, bf16[64,768]{1,0:T(8,128)(2,1)S(1)} %copy-done.1, ...), custom_call_target="tpu_custom_call" | custom-call | tf_op jit(solution)/shard_map/pallas_call | solution.py:264
  24.7 1.2 %shard_map.96 = (f32[768,500]{1,0:T(8,128)S(1)}, f32[8,500]{1,0:T(8,128)}) custom-call(f32[32,768]{1,0:T(8,128)S(1)} %get-tuple-element.4.mt_ref, f32[32,512]{1,0:T(8,128)S(1)} %get-tuple-element.5.r_ref), custom_call_target="tpu_custom_call" | custom-call | tf_op jit(solution)/shard_map/pallas_call | solution.py:299
  25.8 1.6 %copy.12 = f32[768,500]{0,1:T(8,128)} copy(f32[768,500]{1,0:T(8,128)S(1)} %get-tuple-element.6) | data formatting | bytes 3072000 | tf_op jit(solution)/shard_map/pallas_call | solution.py:299
Async XLA Ops:
  1.8 2.0 %copy-start = (bf16[768,768]{1,0:T(8,128)(2,1)S(1)}, bf16[768,768]{1,0:T(8,128)(2,1)}, u32[]{:S(2)}) copy-start(bf16[768,768]{1,0:T(8,128)(2,1)} %centres_hbm.1) | copy-start | bytes 3538948
  1.8 2.0 %copy-start.1 = (bf16[64,768]{1,0:T(8,128)(2,1)S(1)}, bf16[64,768]{1,0:T(8,128)(2,1)}, u32[]{:S(2)}) copy-start(bf16[64,768]{1,0:T(8,128)(2,1)} %pool_hbm.1) | copy-start | bytes 294916
  1.8 2.0 %copy-start.2 = (bf16[64,500]{1,0:T(8,128)(2,1)S(1)}, bf16[64,500]{1,0:T(8,128)(2,1)}, u32[]{:S(2)}) copy-start(bf16[64,500]{1,0:T(8,128)(2,1)} %labels_hbm.1) | copy-start | bytes 192004
  1.8 2.0 %copy-start.3 = (s32[512]{0:T(512)S(1)}, s32[512]{0:T(512)}, u32[]{:S(2)}) copy-start(s32[512]{0:T(512)} %param.13) | copy-start | bytes 6148
  1.9 2.0 %copy-start.4 = (f32[160]{0:T(256)S(1)}, f32[160]{0:T(256)}, u32[]{:S(2)}) copy-start(f32[160]{0:T(256)} %param.15) | copy-start | bytes 1924
  1.9 2.0 %copy-start.5 = (s32[4,1]{0,1:T(1,128)S(1)}, s32[4,1]{0,1:T(1,128)}, u32[]{:S(2)}) copy-start(s32[4,1]{0,1:T(1,128)} %param.12) | copy-start | bytes 52

commit v2 on v1

--- a/solution.py
+++ b/solution.py
@@ -12,7 +12,7 @@
 F32, BF16, I32 = jnp.float32, jnp.bfloat16, jnp.int32
 LANES = 128
 ROWS_PER_STEP = 8
-VMEM_BYTES = 40 * 1024 * 1024
+VMEM_BYTES = 60 * 1024 * 1024
 
 NN = (((1,), (0,)), ((), ()))
 NT = (((1,), (1,)), ((), ()))
@@ -74,8 +74,8 @@
 
     total = steps * shards
     count, width = centres.shape
-    outs = weights.shape[1]
-    eigs = eig.shape[1]
+    outs = weights.shape[0]
+    eigs = eig.shape[0]
     pool_rows = pool.shape[0]
     pieces = width // LANES
     half = x.shape[2]
@@ -114,7 +114,8 @@
     marks = lidx.shape[1]
     chosen = jnp.where(iota((count, marks), 0) == lidx[...], 1.0, 0.0).astype(BF16)
     eig_head, eig_rest = split(eig[...])
-    placed = dot(chosen, eig_head, NN) + dot(chosen, eig_rest, NN)
+    placed = dot(jnp.concatenate([eig_head, eig_rest], axis=0), chosen, NT)
+    placed = placed[:eigs] + placed[eigs:]
     e_parts = split(placed)
     e_head[...], e_rest[...] = e_parts
 
@@ -163,8 +164,8 @@
     kernel = jnp.exp(jnp.sqrt(squared) * (-1.0 / spread))
 
     k_parts = split(kernel)
-    x_w = dot_split(k_parts, (w_head[...], w_rest[...]), NN) - label_rows
-    x_e = dot_split(k_parts, (e_head[...], e_rest[...]), NN)
+    x_w = dot_split(k_parts, (w_head[...], w_rest[...]), NT) - label_rows
+    x_e = dot_split(k_parts, (e_head[...], e_rest[...]), NT)
     x_k = dot_split(k_parts, k_parts, NT)
     for s in range(steps):
         rows = slice(shards * s, shards * (s + 1))
@@ -218,7 +219,7 @@
     gram = rights[:, b_col:b_col + total]
     scaled = split(coeffs * scale[...])
     coupling = (gram - dot_split(scaled, split(coeffs), NT)) * step_size
-    mt_ref[...] = kernel - dot_split(scaled, (e_head[...], e_rest[...]), NT)
+    mt_ref[...] = kernel - dot_split(scaled, (e_head[...], e_rest[...]), NN)
 
     rests = [
         jnp.concatenate([left[s], right[s][:, :w_cols - half]], axis=1) for s in range(steps)
@@ -238,8 +239,8 @@
     m_head, m_rest = split(mt_ref[...])
     r_all = r_ref[...][:, :outs]
     r_head, r_rest = split(r_all)
-    lhs = jnp.concatenate([m_head, m_rest, m_head], axis=0)
-    rhs = jnp.concatenate([r_head, r_head, r_rest], axis=0)
+    lhs = jnp.concatenate([r_head, r_rest, r_head], axis=0)
+    rhs = jnp.concatenate([m_head, m_head, m_rest], axis=0)
     descent_ref[...] = dot(lhs, rhs, TN)
     residual_ref[...] = r_all[last:]
 
@@ -273,14 +274,14 @@
             pltpu.VMEM((1, marks), I32),
             pltpu.VMEM((1, eigs), F32),
             pltpu.VMEM((count, width), BF16),
-            pltpu.VMEM((count, outs), F32),
+            pltpu.VMEM((outs, count), F32),
             pltpu.VMEM((pool_rows, width), BF16),
             pltpu.VMEM((pool_rows, outs), BF16),
-            pltpu.VMEM((marks, eigs), F32),
-            pltpu.VMEM((count, outs), BF16),
-            pltpu.VMEM((count, outs), BF16),
-            pltpu.VMEM((count, eigs), BF16),
-            pltpu.VMEM((count, eigs), BF16),
+            pltpu.VMEM((eigs, marks), F32),
+            pltpu.VMEM((outs, count), BF16),
+            pltpu.VMEM((outs, count), BF16),
+            pltpu.VMEM((eigs, count), BF16),
+            pltpu.VMEM((eigs, count), BF16),
             pltpu.VMEM((pack_rows, LANES), BF16),
             pltpu.VMEM((shards, pack_rows, LANES), BF16),
             pltpu.VMEM((shards, ROWS_PER_STEP, half), F32),
@@ -293,14 +294,14 @@
         ),
     )(
         batch_index.reshape(1, steps), landmark_index.reshape(1, marks),
-        eig_scale.reshape(1, eigs), centres, weights, pool_points, pool_labels, eigvecs,
+        eig_scale.reshape(1, eigs), centres, weights.T, pool_points, pool_labels, eigvecs.T,
     )
     block = count // 3 if count % 384 == 0 else count
-    return pl.pallas_call(
+    descent, residual = pl.pallas_call(
         functools.partial(apply_kernel, outs, total - shards),
         grid=(count // block,),
         out_shape=(
-            jax.ShapeDtypeStruct((count, outs), F32),
+            jax.ShapeDtypeStruct((outs, count), F32),
             jax.ShapeDtypeStruct((shards, outs), F32),
         ),
         in_specs=[
@@ -308,11 +309,12 @@
             pl.BlockSpec((total, padded), lambda i: (0, 0)),
         ],
         out_specs=(
-            pl.BlockSpec((block, outs), lambda i: (i, 0)),
+            pl.BlockSpec((outs, block), lambda i: (0, i)),
             pl.BlockSpec((shards, outs), lambda i: (0, 0)),
         ),
         compiler_params=pltpu.CompilerParams(vmem_limit_bytes=VMEM_BYTES),
     )(mt, r)
+    return descent.T, residual
 
 
 def plain_body(

time: 27.6 us -> 25.4 us (0.920)
  local copies, waits for them, and re-layouts: 4.77 us -> 0 us
  Pallas kernels: 21.9 us -> 24.4 us
    unnamed x14 -> x0, local copies, waits for them, and re-layouts: 3.16 us -> none
    pallas_call x1, Pallas kernels: 1.15 us -> 2.96 us  [fused_body(): pl.pallas_call(functools.partial(apply_kernel, outs, total - shards), gri...]
    pallas_call x1 -> x0, local copies, waits for them, and re-layouts: 1.6 us -> none  [fused_body(): pl.pallas_call(functools.partial(apply_kernel, outs, total - shards), gri...]
    pallas_call x1, Pallas kernels: 20.8 us -> 21.5 us  [fused_body(): pl.pallas_call(functools.partial(steps_kernel, narrow, shards, steps, spr...]
where the time goes in v2:
time: 25.4 us; the launch traced here: 25.1 us
  Pallas kernels  24.4 us (96%)
  between operations  0.64 us (3%)
    pallas_call x1, Pallas kernels, fused_body(): pl.pallas_call(functools.partial(steps_kernel, narrow, shards, steps, spr...  21.5 us
    pallas_call x1, Pallas kernels, fused_body(): pl.pallas_call(functools.partial(apply_kernel, outs, total - shards), gri...  2.96 us

profile of v2, /device:TPU:0, one launch (start us, length us, event | category | flops | bytes accessed | tf_op | source)
XLA Modules:
  0.0 25.1 jit_solution(10574462497430879085)
XLA Ops:
  0.6 21.5 %shard_map.95 = (f32[32,768]{1,0:T(8,128)}, f32[32,512]{1,0:T(8,128)}) custom-call(s32[1,4]{1,0:T(1,128)} %bitcast.10, s32[1,512]{1,0:T(1,128)} %bitcast.8, f32[1,160]{1,0:T(1,128)} %bitcast.9, bf16[768,768]{1,0:T(8,128)(2,1)} %centres_hbm.1, f32[500,768]{1,0:T(8,128)} %bitcast.6, bf16[64,768]{1,0:T(8,128)(2,1)} %pool_hbm.1, bf16[64,500]{1,0:T(8,128)(2,1)} %labels_hbm.1, ...), custom_call_target="tpu_custom_call" | custom-call | tf_op jit(solution)/shard_map/pallas_call | solution.py:265
  22.1 3.0 %shard_map.96 = (f32[500,768]{1,0:T(8,128)}, f32[8,500]{1,0:T(8,128)}) custom-call(f32[32,768]{1,0:T(8,128)} %get-tuple-element.6.mt_ref, f32[32,512]{1,0:T(8,128)} %get-tuple-element.7.r_ref), custom_call_target="tpu_custom_call" | custom-call | tf_op jit(solution)/shard_map/pallas_call | solution.py:300

commit v3 on v2

--- a/solution.py
+++ b/solution.py
@@ -12,7 +12,8 @@
 F32, BF16, I32 = jnp.float32, jnp.bfloat16, jnp.int32
 LANES = 128
 ROWS_PER_STEP = 8
-VMEM_BYTES = 60 * 1024 * 1024
+VMEM_BYTES = 56 * 1024 * 1024
+APPLY_VMEM_BYTES = 16 * 1024 * 1024
 
 NN = (((1,), (0,)), ((), ()))
 NT = (((1,), (1,)), ((), ()))
@@ -42,12 +43,12 @@
 
 def steps_kernel(
     narrow, shards, steps, spread, step_size,
-    bidx_ref, lidx_hbm, scale_hbm, centres_hbm, weights_hbm, pool_hbm, labels_hbm, eig_hbm,
+    bidx_hbm, lidx_hbm, scale_hbm, centres_hbm, weights_hbm, pool_hbm, labels_hbm, eig_hbm,
     mt_ref, r_ref,
-    lidx, scale, centres, weights, pool, labels, eig,
+    bidx_ref, lidx, scale, centres, weights, pool, labels, eig,
     w_head, w_rest, e_head, e_rest,
-    own_pts, all_pts, x, x_in, ag,
-    load_sem, pts_send, pts_recv, x_send, x_recv, ag_send, ag_recv,
+    own_pts, all_pts, ab, ab_in, ab_sum, wx, wx_in, wx_sum,
+    load_sem, pts_send, pts_recv, ab_send, ab_recv, ab_out, ab_back, wx_send, wx_recv, wx_out, wx_back,
 ):
     me = lax.axis_index("wide") * narrow + lax.axis_index("narrow")
     peers = [lax.rem(me + k, shards) for k in range(1, shards)]
@@ -55,12 +56,35 @@
     def at(peer):
         return {"wide": peer // narrow, "narrow": lax.rem(peer, narrow)}
 
+    def remote(src, dst, send, recv, peer, slot):
+        return pltpu.make_async_remote_copy(
+            src_ref=src, dst_ref=dst.at[slot], send_sem=send.at[peer], recv_sem=recv.at[slot],
+            device_id=at(peer), device_id_type=MESH,
+        )
+
+    def send_each(src_of, dst, send, recv):
+        copies = [remote(src_of(peer), dst, send, recv, peer, me) for peer in peers]
+        for copy in copies:
+            copy.start()
+        return copies
+
+    def wait_each(src_of, dst, send, recv):
+        for peer in peers:
+            remote(src_of(peer), dst, send, recv, peer, peer).wait_recv()
+
+    def added(own, slots):
+        terms = [own[pl.ds(me, 1)][0]] + [slots[pl.ds(peer, 1)][0] for peer in peers]
+        while len(terms) > 1:
+            terms = [sum(terms[k:k + 2][1:], terms[k]) for k in range(0, len(terms), 2)]
+        return terms[0]
+
     barrier = pltpu.get_barrier_semaphore()
     for peer in peers:
         pl.semaphore_signal(barrier, inc=1, device_id=at(peer), device_id_type=MESH)
 
     loads = {}
     for place, (name, src, dst) in enumerate((
+        ("bidx", bidx_hbm, bidx_ref),
         ("pool", pool_hbm, pool),
         ("lidx", lidx_hbm, lidx),
         ("eig", eig_hbm, eig),
@@ -78,11 +102,10 @@
     eigs = eig.shape[0]
     pool_rows = pool.shape[0]
     pieces = width // LANES
-    half = x.shape[2]
-    w_cols = 2 * half - 256
-    b_col = w_cols + eigs - half
+    w_half, ab_half = wx.shape[2], ab.shape[2]
 
     loads["pool"].wait()
+    loads["bidx"].wait()
     stacked = jnp.concatenate(
         [pool[:, LANES * q:LANES * (q + 1)] for q in range(pieces)], axis=0
     )
@@ -97,17 +120,10 @@
     own_pts[...] = own.astype(BF16)
 
     pl.semaphore_wait(barrier, shards - 1)
-    pts_copies = []
-    for peer in peers:
-        copy = pltpu.make_async_remote_copy(
-            src_ref=own_pts, dst_ref=all_pts.at[me],
-            send_sem=pts_send.at[peer], recv_sem=pts_recv.at[me],
-            device_id=at(peer), device_id_type=MESH,
-        )
-        copy.start()
-        pts_copies.append(copy)
+    copies = send_each(lambda peer: own_pts, all_pts, pts_send, pts_recv)
     all_pts[pl.ds(me, 1)] = own_pts[...][None]
-    x[...] = jnp.zeros_like(x)
+    ab[...] = jnp.zeros_like(ab)
+    wx[...] = jnp.zeros_like(wx)
 
     loads["lidx"].wait()
     loads["eig"].wait()
@@ -148,14 +164,7 @@
     source = row % shards * pack_rows + row // total * steps + row % total // shards
     order = jnp.where(col == source, 1.0, 0.0).astype(BF16)
 
-    for copy in pts_copies:
-        copy.wait_send()
-    for peer in peers:
-        pltpu.make_async_remote_copy(
-            src_ref=own_pts, dst_ref=all_pts.at[peer],
-            send_sem=pts_send.at[peer], recv_sem=pts_recv.at[peer],
-            device_id=at(peer), device_id_type=MESH,
-        ).wait_recv()
+    wait_each(lambda peer: own_pts, all_pts, pts_send, pts_recv)
     ordered = dot(order, all_pts[...].reshape(shards * pack_rows, LANES), NN)
     points = jnp.concatenate([ordered[total * q:total * (q + 1)] for q in range(pieces)], axis=1)
     point_norms = jnp.sum(points * points, axis=1, keepdims=True)
@@ -164,66 +173,42 @@
     kernel = jnp.exp(jnp.sqrt(squared) * (-1.0 / spread))
 
     k_parts = split(kernel)
-    x_w = dot_split(k_parts, (w_head[...], w_rest[...]), NT) - label_rows
     x_e = dot_split(k_parts, (e_head[...], e_rest[...]), NT)
     x_k = dot_split(k_parts, k_parts, NT)
     for s in range(steps):
         rows = slice(shards * s, shards * (s + 1))
-        x[2 * s] = x_w[rows, :half]
-        x[2 * s + 1, :, :outs - half] = x_w[rows, half:]
-        x[2 * s + 1, :, w_cols - half:b_col] = x_e[rows]
-        x[2 * s + 1, :, b_col:b_col + total] = x_k[rows]
-
-    x_copies = []
-    for peer in peers:
-        copy = pltpu.make_async_remote_copy(
-            src_ref=x.at[peer], dst_ref=x_in.at[me],
-            send_sem=x_send.at[peer], recv_sem=x_recv.at[me],
-            device_id=at(peer), device_id_type=MESH,
-        )
-        copy.start()
-        x_copies.append(copy)
-    summed = x[pl.ds(me, 1)][0]
-    for peer in peers:
-        pltpu.make_async_remote_copy(
-            src_ref=x.at[peer], dst_ref=x_in.at[peer],
-            send_sem=x_send.at[peer], recv_sem=x_recv.at[peer],
-            device_id=at(peer), device_id_type=MESH,
-        ).wait_recv()
-        summed = summed + x_in[pl.ds(peer, 1)][0]
-    ag[pl.ds(me, 1)] = summed[None]
-    ag_copies = []
-    for peer in peers:
-        copy = pltpu.make_async_remote_copy(
-            src_ref=ag.at[me], dst_ref=ag.at[me],
-            send_sem=ag_send.at[peer], recv_sem=ag_recv.at[me],
-            device_id=at(peer), device_id_type=MESH,
-        )
-        copy.start()
-        ag_copies.append(copy)
-    for copy in x_copies:
-        copy.wait_send()
-    for peer in peers:
-        pltpu.make_async_remote_copy(
-            src_ref=ag.at[peer], dst_ref=ag.at[peer],
-            send_sem=ag_send.at[peer], recv_sem=ag_recv.at[peer],
-            device_id=at(peer), device_id_type=MESH,
-        ).wait_recv()
-    for copy in ag_copies:
-        copy.wait_send()
-
-    left = [ag[2 * s] for s in range(steps)]
-    right = [ag[2 * s + 1] for s in range(steps)]
-    rights = jnp.concatenate(right, axis=0)
-    coeffs = rights[:, w_cols - half:b_col]
-    gram = rights[:, b_col:b_col + total]
+        ab[2 * s] = x_e[rows, :ab_half]
+        ab[2 * s + 1, :, :eigs - ab_half] = x_e[rows, ab_half:]
+        ab[2 * s + 1, :, eigs - ab_half:eigs - ab_half + total] = x_k[rows]
+    copies += send_each(lambda peer: ab.at[peer], ab_in, ab_send, ab_recv)
+
+    x_w = dot_split(k_parts, (w_head[...], w_rest[...]), NT) - label_rows
+    for s in range(steps):
+        rows = slice(shards * s, shards * (s + 1))
+        wx[2 * s] = x_w[rows, :w_half]
+        wx[2 * s + 1, :, :outs - w_half] = x_w[rows, w_half:]
+    copies += send_each(lambda peer: wx.at[peer], wx_in, wx_send, wx_recv)
+
+    wait_each(lambda peer: ab.at[peer], ab_in, ab_send, ab_recv)
+    ab_sum[pl.ds(me, 1)] = added(ab, ab_in)[None]
+    copies += send_each(lambda peer: ab_sum.at[me], ab_sum, ab_out, ab_back)
+
+    wait_each(lambda peer: wx.at[peer], wx_in, wx_send, wx_recv)
+    wx_sum[pl.ds(me, 1)] = added(wx, wx_in)[None]
+    copies += send_each(lambda peer: wx_sum.at[me], wx_sum, wx_out, wx_back)
+
+    wait_each(lambda peer: ab_sum.at[peer], ab_sum, ab_out, ab_back)
+    both = jnp.concatenate(
+        [jnp.concatenate([ab_sum[2 * s], ab_sum[2 * s + 1]], axis=1) for s in range(steps)], axis=0
+    )
+    coeffs = both[:, :eigs]
+    gram = both[:, eigs:eigs + total]
     scaled = split(coeffs * scale[...])
     coupling = (gram - dot_split(scaled, split(coeffs), NT)) * step_size
     mt_ref[...] = kernel - dot_split(scaled, (e_head[...], e_rest[...]), NN)
 
-    rests = [
-        jnp.concatenate([left[s], right[s][:, :w_cols - half]], axis=1) for s in range(steps)
-    ]
+    wait_each(lambda peer: wx_sum.at[peer], wx_sum, wx_out, wx_back)
+    rests = [jnp.concatenate([wx_sum[2 * s], wx_sum[2 * s + 1]], axis=1) for s in range(steps)]
     for s in range(steps):
         known = rests[s]
         for later in range(s + 1, steps):
@@ -233,6 +218,8 @@
                 moved = moved - factors[:, j:j + 1] * known[j:j + 1, :]
             rests[later] = moved
         r_ref[shards * s:shards * (s + 1), :] = known
+    for copy in copies:
+        copy.wait_send()
 
 
 def apply_kernel(outs, last, mt_ref, r_ref, descent_ref, residual_ref):
@@ -257,20 +244,19 @@
     spread = math.sqrt(0.5 * width)
     step_size = 32.0 / (count * shards * shards)
     total = steps * shards
-    padded = -(-outs // LANES) * LANES
-    half = (padded + 256) // 2
+    padded = -(-outs // (2 * LANES)) * 2 * LANES
     pack_rows = -(-(steps * width // LANES) // 16) * 16
-    any_spec = pl.BlockSpec(memory_space=pl.ANY)
     vmem_spec = pl.BlockSpec(memory_space=pltpu.VMEM)
     mt, r = pl.pallas_call(
         functools.partial(steps_kernel, narrow, shards, steps, spread, step_size),
         out_shape=(
-            jax.ShapeDtypeStruct((total, count), F32),
-            jax.ShapeDtypeStruct((total, padded), F32),
-        ),
-        in_specs=[pl.BlockSpec(memory_space=pltpu.SMEM)] + [any_spec] * 7,
+            pltpu.VMEM((total, count), F32),
+            pltpu.VMEM((total, padded), F32),
+        ),
+        in_specs=[pl.BlockSpec(memory_space=pltpu.HBM)] * 8,
         out_specs=(vmem_spec, vmem_spec),
         scratch_shapes=[
+            pltpu.SMEM((1, steps), I32),
             pltpu.VMEM((1, marks), I32),
             pltpu.VMEM((1, eigs), F32),
             pltpu.VMEM((count, width), BF16),
@@ -284,11 +270,10 @@
             pltpu.VMEM((eigs, count), BF16),
             pltpu.VMEM((pack_rows, LANES), BF16),
             pltpu.VMEM((shards, pack_rows, LANES), BF16),
-            pltpu.VMEM((shards, ROWS_PER_STEP, half), F32),
-            pltpu.VMEM((shards, ROWS_PER_STEP, half), F32),
-            pltpu.VMEM((shards, ROWS_PER_STEP, half), F32),
-            pltpu.SemaphoreType.DMA((7,)),
-        ] + [pltpu.SemaphoreType.DMA((shards,))] * 6,
+        ] + [pltpu.VMEM((shards, ROWS_PER_STEP, LANES), F32)] * 3
+        + [pltpu.VMEM((shards, ROWS_PER_STEP, padded // 2), F32)] * 3
+        + [pltpu.SemaphoreType.DMA((8,))]
+        + [pltpu.SemaphoreType.DMA((shards,))] * 10,
         compiler_params=pltpu.CompilerParams(
             collective_id=0, has_side_effects=True, vmem_limit_bytes=VMEM_BYTES
         ),
@@ -312,7 +297,7 @@
             pl.BlockSpec((outs, block), lambda i: (0, i)),
             pl.BlockSpec((shards, outs), lambda i: (0, 0)),
         ),
-        compiler_params=pltpu.CompilerParams(vmem_limit_bytes=VMEM_BYTES),
+        compiler_params=pltpu.CompilerParams(vmem_limit_bytes=APPLY_VMEM_BYTES),
     )(mt, r)
     return descent.T, residual
 

time: 25.4 us -> 23 us (0.906)
  Pallas kernels: 24.4 us -> 22.2 us
    pallas_call x1, Pallas kernels: 21.5 us -> 20.1 us  [fused_body(): pl.pallas_call(functools.partial(steps_kernel, narrow, shards, steps, spr...]
    pallas_call x1, Pallas kernels: 2.96 us -> 2.11 us  [fused_body(): pl.pallas_call(functools.partial(apply_kernel, outs, total - shards), gri...]
where the time goes in v3:
time: 23 us; the launch traced here: 22.8 us
  Pallas kernels  22.2 us (97%)
  between operations  0.64 us (3%)
    pallas_call x1, Pallas kernels, fused_body(): pl.pallas_call(functools.partial(steps_kernel, narrow, shards, steps, spr...  20.1 us
    pallas_call x1, Pallas kernels, fused_body(): pl.pallas_call(functools.partial(apply_kernel, outs, total - shards), gri...  2.11 us

profile of v3, /device:TPU:0, one launch (start us, length us, event | category | flops | bytes accessed | tf_op | source)
XLA Modules:
  0.0 22.8 jit_solution(14377333967636376176)
XLA Ops:
  0.6 20.1 %shard_map.95 = (f32[32,768]{1,0:T(8,128)S(1)}, f32[32,512]{1,0:T(8,128)S(1)}) custom-call(s32[1,4]{1,0:T(1,128)} %bitcast.10, s32[1,512]{1,0:T(1,128)} %bitcast.8, f32[1,160]{1,0:T(1,128)} %bitcast.9, bf16[768,768]{1,0:T(8,128)(2,1)} %centres_hbm.1, f32[500,768]{1,0:T(8,128)} %bitcast.6, bf16[64,768]{1,0:T(8,128)(2,1)} %pool_hbm.1, ...), custom_call_target="tpu_custom_call" | custom-call | tf_op jit(solution)/shard_map/pallas_call | solution.py:250
  20.7 2.1 %shard_map.96 = (f32[500,768]{1,0:T(8,128)}, f32[8,500]{1,0:T(8,128)}) custom-call(f32[32,768]{1,0:T(8,128)S(1)} %get-tuple-element.6.mt_ref, f32[32,512]{1,0:T(8,128)S(1)} %get-tuple-element.7.r_ref), custom_call_target="tpu_custom_call" | custom-call | tf_op jit(solution)/shard_map/pallas_call | solution.py:285
